TPU v7x, 32 devices: a whole 2x2x4 slice. The times are simulated.
32 devices in a mesh: dp: 8 (over z, y), seq: 4 (over x, core).
Axes of the slice: x: 2, y: 2, z: 4, core: 2. Of those that a mesh axis runs over, the one named last changes fastest.
Arguments:
- inputs: bfloat16 [16, 1024, 1280], P('dp', 'seq'), may hold values from -6 to 6
- w_query: bfloat16 [1280, 1280], P(('dp', 'seq')), may hold values from -0.15625 to 0.15625
- w_key: bfloat16 [1280, 1280], P(('dp', 'seq')), may hold values from -0.15625 to 0.15625
- w_value: bfloat16 [1280, 1280], P(('dp', 'seq')), may hold values from -0.15625 to 0.15625
- w_out: bfloat16 [1280, 1280], P(('dp', 'seq')), may hold values from -0.625 to 0.625
- w_up: bfloat16 [1280, 1280], P(('dp', 'seq')), may hold values from -0.15625 to 0.15625
- w_down: bfloat16 [1280, 1280], P(('dp', 'seq')), may hold values from -0.3125 to 0.3125
- gain_attn: bfloat16 [1280], P(('dp', 'seq')), may hold values from 0.099609375 to 1.8984375
- gain_mlp: bfloat16 [1280], P(('dp', 'seq')), may hold values from 0.099609375 to 1.8984375
- pad_patches: int32 [16], P('dp'), may hold values from 0 to 1023, as said below
- cotangent: bfloat16 [16, 1024, 1280], P('dp', 'seq'), may hold values from -6 to 6
Outputs:
- layer_out: bfloat16 [16, 1024, 1280], P('dp', 'seq')
- grad_input: float32 [16, 1024, 1280], P('dp', 'seq')
- grad_query: float32 [1280, 1280], P(('dp', 'seq'))
- grad_key: float32 [1280, 1280], P(('dp', 'seq'))
- grad_value: float32 [1280, 1280], P(('dp', 'seq'))
- grad_outproj: float32 [1280, 1280], P(('dp', 'seq'))
- grad_upproj: float32 [1280, 1280], P(('dp', 'seq'))
- grad_downproj: float32 [1280, 1280], P(('dp', 'seq'))
- grad_gain_attn: float32 [1280], P(('dp', 'seq'))
- grad_gain_mlp: float32 [1280], P(('dp', 'seq'))
Inputs may be any that keep to these rules, and one draw needn't show every extreme that they name: `pad_patches`: in each group of 2 contexts held by one index of dp, one context has fewer than 256 padding patches. Some context has no padding and some has 1023 padding patches.
All inputs are finite; a program needn't handle non-finite values.
Results may differ from a plain program's by a relative error of at most 0.03.
Values may be sent and summed in bfloat16 or wider, within the bound.
A program may use at most 256 MiB of HBM per device.

v0:
```python
import functools

import jax
import jax.numpy as jnp
import numpy as np
from jax import lax
from jax.experimental import pallas as pl
from jax.experimental.pallas import tpu as pltpu
from jax.sharding import PartitionSpec as P

HEADS = 16
HEAD_DIM = 80


def shifted(value, axis, steps):
    count = lax.axis_size(axis)
    initial, last = (max(0, -steps), min(count, count - steps))
    return lax.ppermute(value, axis, [(source, source + steps) for source in range(initial, last)])


def rms_scale(values):
    return lax.rsqrt(jnp.mean(values * values, axis=-1, keepdims=True) + 1e-06)


def rms_back(values, scale, gain, grad_norm):
    scaled_grad = grad_norm * gain
    grad_gain = jnp.sum(grad_norm * values * scale, axis=0)
    grad_values = scale * scaled_grad - values * (scale * scale * scale) * jnp.mean(
        scaled_grad * values, axis=-1, keepdims=True
    )
    return (grad_values, grad_gain)


def rope_tables(positions, half):
    freqs = 10000.0 ** (-jnp.arange(half, dtype=jnp.float32) / half)
    angles = positions[:, None].astype(jnp.float32) * freqs[None, :]
    return (jnp.cos(angles), jnp.sin(angles))


def rotate_pairs(tensor, cosine, sine):
    half = tensor.shape[-1] // 2
    first = tensor[..., :half]
    second = tensor[..., half:]
    cos_b = cosine[None, :, None, :]
    sin_b = sine[None, :, None, :]
    return jnp.concatenate(
        [first * cos_b - second * sin_b, first * sin_b + second * cos_b], axis=-1
    )


def rotate_back(tensor, cosine, sine):
    half = tensor.shape[-1] // 2
    first = tensor[..., :half]
    second = tensor[..., half:]
    cos_b = cosine[None, :, None, :]
    sin_b = sine[None, :, None, :]
    return jnp.concatenate(
        [first * cos_b + second * sin_b, second * cos_b - first * sin_b], axis=-1
    )


def block_weights(queries, key_block, source, positions, pad_patches, patches):
    scale_factor = queries.shape[-1] ** (-0.5)
    scores = scale_factor * jnp.einsum(
        "sqhd,skhd->shqk", queries, key_block, preferred_element_type=jnp.float32
    )
    key_pos = source * patches + jnp.arange(patches, dtype=jnp.int32)
    key_grid = key_pos[None, None, :]
    query_grid = positions[None, :, None]
    allowed = (
        (key_grid <= query_grid)
        & ((key_grid >= pad_patches[:, None, None]) | (key_grid == query_grid))
        & (source >= 0)
    )
    allowed = allowed[:, None]
    masked = jnp.where(allowed, scores, -1e30)
    peaks = jnp.max(masked, axis=-1)
    expo = jnp.exp(masked - peaks[..., None]) * allowed.astype(jnp.float32)
    return (expo, peaks)


def block_forward(queries, key_block, value_block, source, positions, pad_patches, patches):
    expo, peaks = block_weights(queries, key_block, source, positions, pad_patches, patches)
    masses = jnp.sum(expo, axis=-1)
    partials = jnp.einsum(
        "shqk,skhd->sqhd",
        expo.astype(jnp.bfloat16),
        value_block,
        preferred_element_type=jnp.float32,
    )
    return (peaks, masses, partials)


def block_backward(
    queries,
    key_block,
    value_block,
    source,
    positions,
    pad_patches,
    patches,
    summit,
    total,
    delta,
    grad_attn,
):
    expo, peaks = block_weights(queries, key_block, source, positions, pad_patches, patches)
    share = jnp.exp(peaks - summit) / total
    share_tok = jnp.swapaxes(share, 1, 2)[..., None]
    grad_part = (share_tok * grad_attn).astype(jnp.bfloat16)
    grad_vblock = jnp.einsum(
        "shqk,sqhd->skhd", expo.astype(jnp.bfloat16), grad_part, preferred_element_type=jnp.float32
    )
    grad_prob = jnp.einsum(
        "sqhd,skhd->shqk", grad_part, value_block, preferred_element_type=jnp.float32
    )
    grad_scores = (expo * (grad_prob - (share * delta)[..., None])).astype(jnp.bfloat16)
    grad_qblock = jnp.einsum(
        "shqk,skhd->sqhd", grad_scores, key_block, preferred_element_type=jnp.float32
    )
    grad_kblock = jnp.einsum(
        "shqk,sqhd->skhd", grad_scores, queries, preferred_element_type=jnp.float32
    )
    return (grad_qblock, grad_kblock, grad_vblock)


MESH_ID = pl.DeviceIdType.MESH
PIECES = ((0, 48, 384), (48, 32, 256))


def coordinates():
    dp = lax.axis_index("dp")
    seq = lax.axis_index("seq")
    return (dp // 2, lax.rem(dp, 2), seq // 2, lax.rem(seq, 2))


def device(z, y, x, c):
    return (z * 2 + y, x * 2 + c)


def peers_of(z, y, x, c):
    along = [device(lax.rem(z + k, 4), y, x, c) for k in (1, 2, 3)]
    return along + [device(z, 1 - y, x, c), device(z, y, 1 - x, c), device(z, y, x, 1 - c)]


def greet(peers):
    barrier = pltpu.get_barrier_semaphore()
    for peer in peers:
        pl.semaphore_signal(barrier, inc=1, device_id=peer, device_id_type=MESH_ID)
    pl.semaphore_wait(barrier, len(peers))


def remote(src, dst, sems, peer):
    return pltpu.make_async_remote_copy(
        src_ref=src,
        dst_ref=dst,
        send_sem=sems[0],
        recv_sem=sems[1],
        device_id=peer,
        device_id_type=MESH_ID,
    )


def send(src, dst, sems, peer):
    copy = remote(src, dst, sems, peer)
    copy.start()
    return copy


class Gather:
    def __init__(self, ref, piece, sems, where):
        first, count, cut = piece
        self.ref, self.sems, self.where = ref, sems, where
        self.rows = pl.ds(first, count)
        self.low, self.high = pl.ds(0, cut), pl.ds(cut, ref.shape[-1] - cut)
        self.copies = [[], [], []]
        self.phase = 0

    def sem(self, i):
        return (self.sems[0].at[i], self.sems[1].at[i])

    def start(self):
        z, y, x, c = self.where
        ref, rows, low, high = self.ref, self.rows, self.low, self.high
        phase = self.phase
        made = []
        if phase == 0:
            block = ref.at[z, y, x, rows, low]
            for k in (1, 2, 3):
                made.append(send(block, block, self.sem(k - 1), device(lax.rem(z + k, 4), y, x, c)))
            block = ref.at[z, y, x, rows, high]
            made.append(send(block, block, self.sem(3), device(z, y, 1 - x, c)))
        elif phase == 1:
            block = ref.at[:, y, x, rows, low]
            made.append(send(block, block, self.sem(4), device(z, 1 - y, x, c)))
            block = ref.at[z, y, :, rows, high]
            for k in (1, 2, 3):
                made.append(send(block, block, self.sem(4 + k), device(lax.rem(z + k, 4), y, x, c)))
        else:
            block = ref.at[:, :, x, rows, low]
            made.append(send(block, block, self.sem(8), device(z, y, 1 - x, c)))
            block = ref.at[:, y, :, rows, high]
            made.append(send(block, block, self.sem(9), device(z, 1 - y, x, c)))
        self.copies[phase] = made
        self.phase = phase + 1

    def arrive(self, phase):
        for copy in self.copies[phase]:
            copy.wait_recv()

    def sent(self):
        for made in self.copies:
            for copy in made:
                copy.wait_send()


HEADS_HERE = 8
SPAN = 256
OFFSETS = (0, 256, 768, 1536, 2560)
NT = (((1,), (1,)), ((), ()))
TN = (((0,), (0,)), ((), ()))


def dot(a, b, dims=(((1,), (0,)), ((), ()))):
    return lax.dot_general(a, b, dims, preferred_element_type=jnp.float32)


def unpack_gains(tiles):
    rows = []
    for z in range(4):
        for y in range(2):
            for x in range(2):
                for c in range(2):
                    rows.append(tiles[z, y, x, c][:, :40])
    full = jnp.concatenate(rows, axis=1)
    return full[0:1], full[1:2]


def spread_heads(value, place):
    for g in range(4):
        pair = dot(value[:, 128 * g : 128 * g + 256], place[g])
        yield pair[:, :128]
        yield pair[:, 128:]


def join_heads(pairs, place):
    wide = [dot(pair, place[g], NT) for g, pair in enumerate(pairs)]
    tiles = [wide[0][:, :128]]
    for g in range(1, 4):
        tiles.append(wide[g - 1][:, 128:] + wide[g][:, :128])
    tiles.append(wide[3][:, 128:])
    return jnp.concatenate(tiles, axis=1)


def join_some(pairs, place, part):
    wide = {g: dot(pair, place[g], NT) for g, pair in pairs.items()}
    if part == 0:
        return jnp.concatenate([wide[0][:, :128], wide[0][:, 128:] + wide[1][:, :128]], axis=1)
    middle = [wide[g - 1][:, 128:] + wide[g][:, :128] for g in (2, 3)]
    return jnp.concatenate(middle + [wide[3][:, 128:]], axis=1)


def forward_kernel(*refs):
    (inputs, cot), weights, tile, pads, cos_ref, sin_ref, places = refs[:2], refs[2:8], refs[8], refs[9], refs[10], refs[11], refs[12]
    (out_qkv, out_wide, tiles, x_own, dy_own, norm_t, out_heads, out_p, out_oh, out_hidden, out_layer, out_slope,
     out_turned, out_down) = refs[13:27]
    (narrow, wide, own, other, held, held_dy, norm, normt, heads, probs, oh, flat, masks, attn, hidden, low_norm, active,
     slope, layer, turned_t,
     ssem, rsem, gs, gr, hs, hr, xs, osem, ws, wr, ns, nr, ls, ps, als, alr, gives, giver, give, extra, total) = refs[27:]
    where = coordinates()
    z, y, x, c = where
    f32, low = jnp.float32, jnp.bfloat16
    across, sibling = device(z, y, 1 - x, c), device(z, y, x, 1 - c)
    keep = pltpu.make_async_copy(inputs.at[x], held.at[x], ls.at[0])
    keep.start()
    keep_dy = pltpu.make_async_copy(cot.at[x], held_dy.at[x], ls.at[1])
    keep_dy.start()
    greet(peers_of(*where))
    for w in range(6):
        for h in range(2):
            own[h, w] = weights[w][:, 640 * h : 640 * h + 640].astype(f32)
    tiles[z, y, x, c] = tile[...]
    pair = send(own.at[1 - c], other, (xs.at[0], xs.at[1]), sibling)
    pair_tile = send(tiles.at[z, y, x, c], tiles.at[z, y, x, c], (xs.at[2], xs.at[3]), sibling)
    pair.wait_recv()
    pair_tile.wait_recv()
    steps, shares, stores, sends = [], {}, [], [pair, pair_tile]

    def place(w):
        return narrow.at[w] if w < 3 else wide.at[w - 3, c]

    for w in range(6):
        mine, theirs = own[c, w], other[w]
        first = c == 0
        block = jnp.concatenate([jnp.where(first, mine, theirs), jnp.where(first, theirs, mine)], axis=0)
        place(w)[z, y, x] = block.astype(low)
        for i, piece in enumerate(PIECES):
            n = len(steps)
            steps.append(Gather(place(w), piece, (ssem.at[n], rsem.at[n]), where))

    def tile_step(i, block, peers):
        return [send(block, block, (gs.at[i + j], gr.at[i + j]), peer) for j, peer in enumerate(peers)]

    state = {"made": tile_step(0, tiles.at[z, y, x], [device(lax.rem(z + k, 4), y, x, c) for k in (1, 2, 3)])}

    def store(src, dst, sem):
        copy = pltpu.make_async_copy(src, dst, sem)
        copy.start()
        stores.append(copy)

    per = len(PIECES)
    count = 6 * per

    def settle(n):
        w, i = n // per, n % per
        if w < 3:
            if i == per - 1:
                store(narrow.at[w], out_qkv.at[w], osem.at[w])
            return
        part = wide.at[w - 3, c, :, :, :, pl.ds(PIECES[i][0], PIECES[i][1])]
        shares.setdefault(w, []).append(send(part, part, (hs.at[n], hr.at[n]), sibling))

    def whole(w):
        for copy in shares[w]:
            copy.wait_recv()
        sends.extend(shares[w])
        store(wide.at[w - 3], out_wide.at[w - 3], osem.at[w])

    swaps = []

    def swap(src, dst):
        n, i = len(swaps), len(swaps) % 4
        rows = pl.ds(64 * i, 64)
        swaps.append(send(src.at[1 - x, rows], dst.at[x, rows], (ws.at[n], wr.at[n]), across))
        sends.append(swaps[n])

    def advance(t):
        if t < count:
            steps[t].start()
        if 0 <= t - 1 < count:
            steps[t - 1].arrive(0)
            steps[t - 1].start()
        if t in (1, 2, 3):
            for m in state["made"]:
                m.wait_recv()
            sends.extend(state["made"])
            state["made"] = []
        if t == 1:
            state["made"] = tile_step(3, tiles.at[:, y, x], [device(z, 1 - y, x, c)])
        if t == 2:
            state["made"] = tile_step(4, tiles.at[:, :, x], [device(z, y, 1 - x, c)])
        if 0 <= t - 2 < count:
            steps[t - 2].arrive(1)
            steps[t - 2].start()
        if t < 3:
            swap(inputs, held)
            if t == 2:
                swap(inputs, held)
        if 5 <= t < 9:
            swap(cot, held_dy)
        if 0 <= t - 3 < count:
            steps[t - 3].arrive(2)
            settle(t - 3)

    advance(0)
    pad = pads[x]
    row = lax.broadcasted_iota(jnp.int32, (SPAN, SPAN), 0)
    col = lax.broadcasted_iota(jnp.int32, (SPAN, SPAN), 1)
    for i in range(4):
        good = (col <= row) & ((col + SPAN * i >= pad) | (col == row))
        masks[i] = jnp.where(good, 0.0, -1e30).astype(f32)
    before = jnp.where(lax.broadcasted_iota(jnp.int32, (1, 3 * SPAN), 1) >= pad, 0.0, -1e30).astype(f32)
    advance(1)
    advance(2)
    advance(3)
    keep.wait()
    for copy in swaps:
        copy.wait_recv()
    gain_attn, gain_mlp = unpack_gains(tiles)
    passed = []
    for j in range(2):
        value = held[j].astype(f32)
        scale = lax.rsqrt(jnp.mean(value * value, axis=-1, keepdims=True) + 1e-06)
        block = 2 * j + c
        norm[block] = (value * scale * gain_attn).astype(low)
        passed.append(send(norm.at[block], norm.at[block], (ns.at[j], nr.at[j]), sibling))
    store(held, x_own, ls.at[2])
    sends.extend(passed)
    advance(4)
    for copy in passed:
        copy.wait_recv()

    def project(t):
        def step(b, _):
            rows = pl.ds(pl.multiple_of(b * SPAN, SPAN), SPAN)
            value = dot(norm[b], narrow[t].reshape(1280, 640)).astype(low)
            plain = spread_heads(value, places.at[0])
            if t < 2:
                cosine, sine = cos_ref[rows, :], sin_ref[rows, :]
                if t == 0:
                    cosine, sine = cosine * (80.0**-0.5), sine * (80.0**-0.5)
                for h, (one, two) in enumerate(zip(plain, spread_heads(value, places.at[1]))):
                    heads[t, h, rows, :] = (one * cosine + two * sine).astype(low)
            else:
                for h, one in enumerate(plain):
                    heads[t, h, rows, :] = one.astype(low)
            if t == 0:
                normt[:, rows] = jnp.transpose(norm[b])
            return 0

        lax.fori_loop(0, 4, step, 0)

    project(0)
    store(normt, norm_t, ls.at[3])
    advance(5)
    advance(6)
    project(1)
    advance(7)
    advance(8)
    project(2)
    store(heads, out_heads, ls.at[4])

    def attend(h, _):
        slot = lax.rem(h, 2)

        @pl.when(h >= 2)
        def _():
            pltpu.make_async_copy(probs.at[slot], out_p.at[h - 2], ps.at[slot]).wait()

        for i in range(4):
            n = SPAN * (i + 1)
            rows = slice(SPAN * i, SPAN * i + SPAN)
            score = dot(heads[0, h, rows, :], heads[1, h, :n, :], NT)
            last = score[:, n - SPAN :] + masks[i]
            score = last if i == 0 else jnp.concatenate([score[:, : n - SPAN] + before[:, : n - SPAN], last], axis=1)
            peak = jnp.max(score, axis=-1, keepdims=True)
            expo = jnp.exp(score - peak)
            share = (expo * (1.0 / jnp.sum(expo, axis=-1, keepdims=True))).astype(low)
            probs[slot, :, OFFSETS[i] : OFFSETS[i + 1]] = share
            oh[h, rows, :] = dot(share, heads[2, h, :n, :]).astype(low)
        pltpu.make_async_copy(probs.at[slot], out_p.at[h], ps.at[slot]).start()
        return 0

    lax.fori_loop(0, 2, attend, 0)
    advance(9)
    lax.fori_loop(2, 4, attend, 0)
    advance(10)
    lax.fori_loop(4, 6, attend, 0)
    advance(11)
    lax.fori_loop(6, 8, attend, 0)
    store(oh, out_oh, ls.at[5])

    def flatten(b, _):
        rows = pl.ds(pl.multiple_of(b * SPAN, SPAN), SPAN)
        pairs = [jnp.concatenate([oh[2 * g, rows, :], oh[2 * g + 1, rows, :]], axis=1) for g in range(4)]
        flat[b] = join_heads(pairs, places.at[0]).astype(low)
        return 0

    lax.fori_loop(0, 4, flatten, 0)
    columns = pl.ds(pl.multiple_of(640 * c, 128), 640)
    joined = []
    for j in range(2):
        attn[j, :, columns] = flat[2 * j + c]
        joined.append(send(flat.at[2 * j + 1 - c], attn.at[j, :, columns], (als.at[j], alr.at[j]), sibling))
    sends.extend(joined)
    advance(12)
    for copy in joined:
        copy.wait_recv()
    whole(3)

    def out_step(j, _):
        rows = pl.ds(pl.multiple_of(j * SPAN, SPAN), SPAN)
        for h in range(2):
            lanes = slice(640 * h, 640 * h + 640)
            branch = dot(attn[j], wide[0, h].reshape(1280, 640))
            hidden[j, :, lanes] = held[j, :, lanes].astype(f32) + branch
        value = hidden[j]
        scale = lax.rsqrt(jnp.mean(value * value, axis=-1, keepdims=True) + 1e-06)
        low_norm[j] = (value * scale * gain_mlp).astype(low)
        turned_t[0, :, rows] = jnp.transpose(attn[j])
        turned_t[1, :, rows] = jnp.transpose(low_norm[j])
        return 0

    lax.fori_loop(0, 2, out_step, 0)
    store(hidden, out_hidden, ls.at[6])
    advance(13)
    whole(4)

    def up_step(j, _):
        rows = pl.ds(pl.multiple_of(j * SPAN, SPAN), SPAN)
        for h in range(2):
            lanes = slice(640 * h, 640 * h + 640)
            upper = dot(low_norm[j], wide[1, h].reshape(1280, 640))
            gate = 1.0 / (1.0 + jnp.exp(-upper))
            active[j, :, lanes] = (upper * gate).astype(low)
            slope[j, :, lanes] = (gate * (1.0 + upper * (1.0 - gate))).astype(low)
        turned_t[2, :, rows] = jnp.transpose(active[j])
        return 0

    lax.fori_loop(0, 2, up_step, 0)
    store(slope, out_slope, ls.at[7])
    store(turned_t, out_turned, ls.at[8])
    for copy in swaps[4:]:
        copy.wait_recv()
    keep_dy.wait()
    store(held_dy, dy_own, ls.at[9])
    yours = pl.ds(pl.multiple_of(640 * (1 - c), 128), 640)

    def grad_step(zi, half, ref):
        rows = pl.ds(pl.multiple_of(zi * 320, 320), 320)
        value = dot(turned_t[2, rows, :256], held_dy[0, :, half]) + dot(turned_t[2, rows, 256:], held_dy[1, :, half])
        ref[zi] = value.astype(low).reshape(2, 2, 80, 640)
        return 0

    lax.fori_loop(0, 4, lambda zi, _: grad_step(zi, yours, give), 0)
    given = send(give, extra, (gives.at[0], giver.at[0]), sibling)
    sends.append(given)
    advance(14)
    lax.fori_loop(0, 4, lambda zi, _: grad_step(zi, columns, total), 0)
    given.wait_recv()

    def fold(i, _):
        zi, yi = i // 2, lax.rem(i, 2)
        for xi in range(2):
            total[zi, yi, xi] = (total[zi, yi, xi].astype(f32) + extra[zi, yi, xi].astype(f32)).astype(low)
        return 0

    lax.fori_loop(0, 8, fold, 0)
    store(total, out_down, ls.at[11])
    whole(5)

    def down_step(j, _):
        for h in range(2):
            lanes = slice(640 * h, 640 * h + 640)
            value = hidden[j, :, lanes] + dot(active[j], wide[2, h].reshape(1280, 640))
            layer[j, :, lanes] = value.astype(low)
        return 0

    lax.fori_loop(0, 2, down_step, 0)
    store(layer, out_layer, ls.at[10])
    for h in (6, 7):
        pltpu.make_async_copy(probs.at[h % 2], out_p.at[h], ps.at[h % 2]).wait()
    for item in steps:
        item.sent()
    for copy in sends:
        copy.wait_send()
    for copy in stores:
        copy.wait()


def forward_part(inputs, cot, weights, tile, pads, cosine, sine, places):
    dma = pltpu.SemaphoreType.DMA
    low, f32 = jnp.bfloat16, jnp.float32
    shape = jax.ShapeDtypeStruct
    vmem, anywhere = pl.BlockSpec(memory_space=pltpu.VMEM), pl.BlockSpec(memory_space=pl.ANY)
    tokens = (2, 256, 1280)
    n = 6 * len(PIECES)
    return pl.pallas_call(
        forward_kernel,
        name="gather_forward",
        out_shape=(
            shape((3, 4, 2, 2, 80, 640), low),
            shape((3, 2, 4, 2, 2, 80, 640), low),
            shape((4, 2, 2, 2, 8, 128), f32),
            shape(tokens, low),
            shape(tokens, low),
            shape((1280, 1024), low),
            shape((3, 8, 1024, 128), low),
            shape((8, 256, 2560), low),
            shape((8, 1024, 128), low),
            shape(tokens, f32),
            shape(tokens, low),
            shape(tokens, low),
            shape((3, 1280, 512), low),
            shape((4, 2, 2, 80, 640), low),
        ),
        in_specs=[anywhere] * 2 + [vmem] * 7 + [pl.BlockSpec(memory_space=pltpu.SMEM)] + [vmem] * 3,
        out_specs=(anywhere,) * 2 + (vmem,) + (anywhere,) * 11,
        scratch_shapes=[
            pltpu.VMEM((3, 4, 2, 2, 80, 640), low),
            pltpu.VMEM((3, 2, 4, 2, 2, 80, 640), low),
            pltpu.VMEM((2, 6, 40, 640), f32),
            pltpu.VMEM((6, 40, 640), f32),
            pltpu.VMEM(tokens, low),
            pltpu.VMEM(tokens, low),
            pltpu.VMEM((4, 256, 1280), low),
            pltpu.VMEM((1280, 1024), low),
            pltpu.VMEM((3, 8, 1024, 128), low),
            pltpu.VMEM((2, 256, 2560), low),
            pltpu.VMEM((8, 1024, 128), low),
            pltpu.VMEM((4, 256, 640), low),
            pltpu.VMEM((4, 256, 256), f32),
            pltpu.VMEM(tokens, low),
            pltpu.VMEM(tokens, f32),
            pltpu.VMEM(tokens, low),
            pltpu.VMEM(tokens, low),
            pltpu.VMEM(tokens, low),
            pltpu.VMEM(tokens, low),
            pltpu.VMEM((3, 1280, 512), low),
            dma((n, 10)), dma((n, 10)), dma((5,)), dma((5,)), dma((n,)), dma((n,)), dma((4,)), dma((6,)),
            dma((8,)), dma((8,)), dma((2,)), dma((2,)), dma((12,)), dma((2,)), dma((2,)), dma((2,)),
            dma((1,)), dma((1,)),
        ] + [pltpu.VMEM((4, 2, 2, 80, 640), low)] * 3 + [
        ],
        compiler_params=pltpu.CompilerParams(
            collective_id=0, has_side_effects=True, vmem_limit_bytes=60 << 20
        ),
    )(inputs, cot, *weights, tile, pads, cosine, sine, places)


class Scatter:
    def __init__(self, ref, piece, bufs, sems, where):
        first, count, cut = piece
        self.ref, self.cut, self.bufs, self.sems, self.where = ref, cut, bufs, sems, where
        self.rows = pl.ds(first, count)
        self.low, self.high = pl.ds(0, cut), pl.ds(cut, ref.shape[-1] - cut)
        self.copies = []
        self.next = []
        self.stage = 0

    def sem(self, i):
        return (self.sems[0].at[i], self.sems[1].at[i])

    def post(self, makers):
        self.next = makers
        self.copies += makers
        for maker in makers:
            maker().start()

    def arrive(self):
        for maker in self.next:
            maker().wait_recv()

    def start(self):
        z, y, x, c = self.where
        ref, b, rows = self.ref, self.bufs, self.rows
        self.post([
            lambda: remote(ref.at[:, :, 1 - x, rows, self.low], b["a1"], self.sem(0), device(z, y, 1 - x, c)),
            lambda: remote(ref.at[:, 1 - y, :, rows, self.high], b["b1"], self.sem(1), device(z, 1 - y, x, c)),
        ])

    def second(self):
        z, y, x, c = self.where
        ref, b, rows, wide, thin = self.ref, self.bufs, self.rows, self.low, self.high
        f32, low = jnp.float32, jnp.bfloat16
        self.arrive()

        def fold(i, _):
            zi, yi = i // 2, lax.rem(i, 2)
            ref[zi, yi, x, rows, wide] = (ref[zi, yi, x, rows, wide].astype(f32) + b["a1"][zi, yi].astype(f32)).astype(low)
            ref[zi, y, yi, rows, thin] = (ref[zi, y, yi, rows, thin].astype(f32) + b["b1"][zi, yi].astype(f32)).astype(low)
            return 0

        lax.fori_loop(0, 8, fold, 0)
        def along(k):
            other = lax.rem(z + k, 4)
            return remote(ref.at[other, y, :, rows, thin], b["b2"].at[k - 1], self.sem(2 + k), device(other, y, x, c))

        made = [lambda: remote(ref.at[:, 1 - y, x, rows, wide], b["a2"], self.sem(2), device(z, 1 - y, x, c))]
        self.post(made + [functools.partial(along, k) for k in (1, 2, 3)])

    def third(self):
        z, y, x, c = self.where
        ref, b, rows, wide, thin = self.ref, self.bufs, self.rows, self.low, self.high
        f32, low = jnp.float32, jnp.bfloat16
        self.arrive()

        def fold(zi, _):
            ref[zi, y, x, rows, wide] = (ref[zi, y, x, rows, wide].astype(f32) + b["a2"][zi].astype(f32)).astype(low)
            return 0

        lax.fori_loop(0, 4, fold, 0)
        value = ref[z, y, 1 - x, rows, thin].astype(f32)
        for k in range(3):
            value = value + b["b2"][k, 1 - x].astype(f32)
        ref[z, y, 1 - x, rows, thin] = value.astype(low)
        def along(k):
            other = lax.rem(z + k, 4)
            return remote(ref.at[other, y, x, rows, wide], b["a3"].at[k - 1], self.sem(6 + k), device(other, y, x, c))

        made = [lambda: remote(ref.at[z, y, 1 - x, rows, thin], b["b3"], self.sem(6), device(z, y, 1 - x, c))]
        self.post(made + [functools.partial(along, k) for k in (1, 2, 3)])

    def finish(self, out):
        z, y, x, c = self.where
        ref, b, rows = self.ref, self.bufs, self.rows
        f32 = jnp.float32
        self.arrive()
        left = ref[z, y, x, rows, self.low].astype(f32)
        right = ref[z, y, x, rows, self.high].astype(f32) + b["b3"][...].astype(f32)
        for k in range(3):
            left = left + b["a3"][k].astype(f32)
            right = right + b["b2"][k, x].astype(f32)
        out[rows, self.low] = left
        out[rows, self.high] = right
        for maker in self.copies:
            maker().wait_send()


def scatter_buffers(piece, columns):
    first, rows, cut = piece
    rest = columns - cut
    return {
        "a1": (4, 2, rows, cut),
        "a2": (4, rows, cut),
        "a3": (3, rows, cut),
        "b1": (4, 2, rows, rest),
        "b2": (3, 2, rows, rest),
        "b3": (rows, rest),
    }


SLOTS = 4
BACK_PIECES = ((0, 80, 384),)


def backward_kernel(*refs):
    (layer, hidden, slope_in, turned_in, down_in, dy_in, wide_in, weights_in, tiles, x_own, norm_t, heads_in, p_in, oh_in,
     cos_ref, sin_ref, places) = refs[:17]
    (out_layer, out_near, out_far, o_q, o_k, o_v, o_o, o_up, o_down, o_ga, o_gm) = refs[17:28]
    (sums, extra, flat_in, xs_own, hid, shown, part_recv, in_recv, fins, finr, tot, trecv, gain_rows,
     ls, es, er, ss, sr, fs, fr, gs, gr, ps, qs, qr, ys, yr, os) = refs[28:56]
    per = len(BACK_PIECES)
    bufs = []
    rest = refs[56:]
    for i in range(per):
        bufs.append(dict(zip(scatter_buffers(BACK_PIECES[i], 640), rest[6 * i : 6 * i + 6])))
    where = coordinates()
    z, y, x, c = where
    f32, low = jnp.float32, jnp.bfloat16
    dma = pltpu.SemaphoreType.DMA
    across, sibling = device(z, y, 1 - x, c), device(z, y, x, 1 - c)
    mine = pl.ds(pl.multiple_of(640 * c, 128), 640)
    yours = pl.ds(pl.multiple_of(640 * (1 - c), 128), 640)
    sends = []

    def local(src, dst, sem):
        copy = pltpu.make_async_copy(src, dst, sem)
        copy.start()
        return copy

    parts = []
    for n in range(6):
        for i, piece in enumerate(BACK_PIECES):
            held = {k: v.at[n] for k, v in bufs[i].items()}
            m = per * n + i
            parts.append(Scatter(sums.at[n % SLOTS], piece, held, (ss.at[m], sr.at[m]), where))
    outs = (o_down, o_up, o_o, o_v, o_k, o_q)
    active, crossing, done = [], [], []

    def pump(*fresh):
        older = list(active)
        for m in fresh:
            parts[m].start()
        active[:0] = fresh
        for m in older:
            part = parts[m]
            part.stage += 1
            if part.stage == 1:
                part.second()
            elif part.stage == 2:
                part.third()
            elif part.stage == 3:
                n = m // per
                part.finish(fins.at[n])
                if m % per == per - 1:
                    theirs = pl.ds(pl.multiple_of(40 * (1 - c), 8), 40)
                    crossing.append((n, send(fins.at[n, theirs], finr.at[n], (fs.at[n], fr.at[n]), sibling)))
            else:
                active.remove(m)
                done.append(m)
                if m % per == per - 1:
                    n = m // per
                    dict(crossing)[n].wait_recv()
                    own = fins[n, pl.ds(pl.multiple_of(40 * c, 8), 40), :]
                    theirs, first = finr[n], c == 0
                    outs[n][:, :640] = jnp.where(first, own, theirs)
                    outs[n][:, 640:] = jnp.where(first, theirs, own)

    def fold(n):
        def step(i, _):
            zi, yi = i // 2, lax.rem(i, 2)
            for xi in range(2):
                value = sums[n, zi, yi, xi].astype(f32) + extra[n, zi, yi, xi].astype(f32)
                sums[n, zi, yi, xi] = value.astype(low)
            return 0

        lax.fori_loop(0, 8, step, 0)

    load_x = local(x_own, xs_own, ls.at[0])
    load_hid = local(hidden, hid, ls.at[1])
    load_shown = local(layer, shown, ls.at[2])

    def feed_forward(turned, dy, slope, wide, grad_upper, hid_low, give, stage):
        load_down = local(down_in, sums.at[0], ls.at[5])
        load_turned = [local(turned_in.at[k], turned.at[k], ls.at[3 + k]) for k in (1, 0)]
        load_dy = local(dy_in, dy, ls.at[6])
        load_wide = [local(wide_in.at[k], wide.at[k], ls.at[7 + k]) for k in (2, 1, 0)]
        load_slope = local(slope_in, slope, ls.at[10])
        greet(peers_of(*where))
        _, gain_mlp = unpack_gains(tiles)
        given = []

        def product(n, k, right):
            def theirs_step(zi, _):
                rows = pl.ds(pl.multiple_of(zi * 320, 320), 320)
                give[n - 1, zi] = dot(turned[k, rows, :], right[:, yours]).astype(low).reshape(2, 2, 80, 640)
                return 0

            lax.fori_loop(0, 4, theirs_step, 0)
            given.append(send(give.at[n - 1], extra.at[n], (es.at[2 + n], er.at[2 + n]), sibling))

            def own_step(zi, _):
                rows = pl.ds(pl.multiple_of(zi * 320, 320), 320)
                sums[n, zi] = dot(turned[k, rows, :], right[:, mine]).astype(low).reshape(2, 2, 80, 640)
                return 0

            lax.fori_loop(0, 4, own_step, 0)

        load_down.wait()
        pump(*range(per))
        load_dy.wait()
        load_wide[0].wait()
        load_slope.wait()

        def active_step(j, _):
            rows = pl.ds(pl.multiple_of(j * SPAN, SPAN), SPAN)
            total = dot(dy[rows, :640], wide[2, 0].reshape(1280, 640), NT)
            total = total + dot(dy[rows, 640:], wide[2, 1].reshape(1280, 640), NT)
            grad_upper[rows, :] = (total * slope[rows, :].astype(f32)).astype(low)
            return 0

        lax.fori_loop(0, 2, active_step, 0)
        load_turned[0].wait()
        product(1, 1, grad_upper)
        load_wide[1].wait()
        load_hid.wait()
        gain_rows[...] = jnp.zeros_like(gain_rows)

        def hidden_step(j, _):
            rows = pl.ds(pl.multiple_of(j * SPAN, SPAN), SPAN)
            grad_norm = dot(grad_upper[rows, :640], wide[1, 0].reshape(1280, 640), NT)
            grad_norm = grad_norm + dot(grad_upper[rows, 640:], wide[1, 1].reshape(1280, 640), NT)
            value = hid[rows, :]
            scale = lax.rsqrt(jnp.mean(value * value, axis=-1, keepdims=True) + 1e-06)
            scaled = grad_norm * gain_mlp
            mean = jnp.mean(scaled * value, axis=-1, keepdims=True)
            gain_rows[0:1] = gain_rows[0:1] + jnp.sum(grad_norm * value * scale, axis=0, keepdims=True)
            result = dy[rows, :].astype(f32) + scale * scaled - value * (scale * scale * scale) * mean
            hid[rows, :] = result
            hid_low[rows, :] = result.astype(low)
            return 0

        lax.fori_loop(0, 2, hidden_step, 0)
        given[0].wait_recv()
        fold(1)
        pump(*range(per, 2 * per))
        load_wide[2].wait()
        moved = []

        def heads_grad(j, half):
            rows = pl.ds(SPAN * j, SPAN)
            total = dot(hid_low[rows, :640], wide[0, 0, pl.ds(2 * half, 2)].reshape(640, 640), NT)
            return total + dot(hid_low[rows, 640:], wide[0, 1, pl.ds(2 * half, 2)].reshape(640, 640), NT)

        for j in range(2):
            stage[j] = heads_grad(j, 1 - c).astype(low)
            moved.append(send(stage.at[j], flat_in.at[2 * j + c], (es.at[j], er.at[j]), sibling))
        for j in range(2):
            flat_in[2 * j + c] = heads_grad(j, c).astype(low)
        load_turned[1].wait()
        product(2, 0, hid_low)
        for copy in moved:
            copy.wait()
        given[1].wait_recv()
        fold(2)
        for copy in given:
            copy.wait_send()

    tokens = (512, 1280)
    pl.run_scoped(
        feed_forward,
        pltpu.VMEM((2, 1280, 512), low),
        pltpu.VMEM(tokens, low),
        pltpu.VMEM(tokens, low),
        pltpu.VMEM((3, 2, 4, 2, 2, 80, 640), low),
        pltpu.VMEM(tokens, low),
        pltpu.VMEM(tokens, low),
        pltpu.VMEM((2, 4, 2, 2, 80, 640), low),
        pltpu.VMEM((2, 256, 640), low),
    )

    def attention(heads, probs, oh, doh, acc, flat, normt, part_send, in_send, in_own):
        def fetch(h, slot):
            return pltpu.make_async_copy(p_in.at[h], probs.at[slot], ps.at[slot])

        load_heads = local(heads_in, heads, ls.at[3])
        fetch(0, 0).start()
        load_oh = local(oh_in, oh, ls.at[4])
        load_normt = local(norm_t, normt, ls.at[5])
        weights = extra
        load_weights = local(weights_in, weights, ls.at[6])
        pump(*range(2 * per, 3 * per))
        load_shown.wait()
        own_layer = local(shown.at[x], out_layer.at[x], ls.at[7])
        back_layer = send(shown.at[1 - x], out_layer.at[x], (ys.at[1], yr.at[1]), across)
        sends.append(back_layer)

        def spread(b, _):
            rows = pl.ds(pl.multiple_of(b * SPAN, SPAN), SPAN)
            for h, one in enumerate(spread_heads(flat_in[b], places.at[0])):
                doh[h, rows, :] = one.astype(low)
            return 0

        lax.fori_loop(0, 4, spread, 0)
        load_heads.wait()
        load_oh.wait()

        def attend(h, _):
            slot = lax.rem(h, 2)

            @pl.when(h < 7)
            def _():
                fetch(h + 1, 1 - slot).start()

            fetch(h, slot).wait()
            for i in range(4):
                n = SPAN * (i + 1)
                rows = slice(SPAN * i, SPAN * i + SPAN)
                grad = doh[h, rows, :]
                delta = jnp.sum(grad.astype(f32) * oh[h, rows, :].astype(f32), axis=-1, keepdims=True)
                share = probs[slot, :, OFFSETS[i] : OFFSETS[i + 1]]
                grad_share = dot(grad, heads[2, h, :n, :], NT)
                grad_score = (share.astype(f32) * (grad_share - delta)).astype(low)
                grad_query = dot(grad_score, heads[1, h, :n, :]) * (80.0**-0.5)
                grad_key = dot(grad_score, heads[0, h, rows, :], TN)
                grad_value = dot(share, grad, TN)
                heads[0, h, rows, :] = grad_query.astype(low)
                if i > 0:
                    acc[0, : n - SPAN] = acc[0, : n - SPAN] + grad_key[: n - SPAN]
                    acc[1, : n - SPAN] = acc[1, : n - SPAN] + grad_value[: n - SPAN]
                acc[0, n - SPAN : n] = grad_key[n - SPAN :]
                acc[1, n - SPAN : n] = grad_value[n - SPAN :]
            heads[1, h] = acc[0].astype(low)
            heads[2, h] = acc[1].astype(low)
            return 0

        lax.fori_loop(0, 5, attend, 0)
        pump()
        lax.fori_loop(5, 8, attend, 0)
        load_normt.wait()

        def product(t, n):
            def join(b, _):
                rows = pl.ds(pl.multiple_of(b * SPAN, SPAN), SPAN)
                pairs = [jnp.concatenate([heads[t, 2 * g, rows, :], heads[t, 2 * g + 1, rows, :]], axis=1) for g in range(4)]
                if t == 2:
                    flat[t, rows, :] = join_heads(pairs, places.at[0]).astype(low)
                    return 0
                total = 0.0
                for move, table in ((0, cos_ref), (1, sin_ref)):
                    twice = jnp.concatenate([table[rows, :], table[rows, :]], axis=1)
                    turned = [(pair.astype(f32) * twice).astype(low) for pair in pairs]
                    total = total + join_heads(turned, places.at[move])
                flat[t, rows, :] = total.astype(low)
                return 0

            lax.fori_loop(0, 4, join, 0)

            def step(zi, _):
                rows = pl.ds(pl.multiple_of(zi * 320, 320), 320)
                sums[n % SLOTS, zi] = dot(normt[rows, :], flat[t]).astype(low).reshape(2, 2, 80, 640)
                return 0

            lax.fori_loop(0, 4, step, 0)

        product(2, 3)
        pump(*range(3 * per, 4 * per))
        product(1, 4)
        pump(*range(4 * per, 5 * per))
        product(0, 5)
        pump(*range(5 * per, 6 * per))
        load_weights.wait()

        def norm_grad(block):
            rows = pl.ds(pl.multiple_of(block * SPAN, SPAN), SPAN)
            total = dot(flat[0, rows, :], weights[0].reshape(1280, 640), NT)
            for t in (1, 2):
                total = total + dot(flat[t, rows, :], weights[t].reshape(1280, 640), NT)
            return total

        def theirs_step(j, _):
            part_send[j] = norm_grad(2 * j + 1 - c).astype(low)
            return 0

        lax.fori_loop(0, 2, theirs_step, 0)
        swapped = [send(part_send.at[j], part_recv.at[j], (qs.at[j], qr.at[j]), sibling) for j in range(2)]
        gain_attn, _ = unpack_gains(tiles)
        load_x.wait()
        for copy in swapped:
            copy.wait_recv()

        def input_grad(j):
            grad_norm = norm_grad(2 * j + c) + part_recv[j].astype(f32)
            value = xs_own[j].astype(f32)
            scale = lax.rsqrt(jnp.mean(value * value, axis=-1, keepdims=True) + 1e-06)
            scaled = grad_norm * gain_attn
            mean = jnp.mean(scaled * value, axis=-1, keepdims=True)
            gain_rows[1:2] = gain_rows[1:2] + jnp.sum(grad_norm * value * scale, axis=0, keepdims=True)
            rows = pl.ds(pl.multiple_of(j * SPAN, SPAN), SPAN)
            return hid[rows, :] + scale * scaled - value * (scale * scale * scale) * mean

        in_send[...] = input_grad(1 - x).astype(low)
        back = send(in_send, in_recv, (ys.at[0], yr.at[0]), across)
        in_own[...] = input_grad(x)
        own_input = local(in_own, out_near, os.at[0])
        both = gain_rows[0:2]
        for p in range(16):
            tot[p // 4, (p // 2) % 2, p % 2, 0:2, 0:80] = both[:, 80 * p : 80 * p + 80]
        hop = [send(tot, trecv.at[0], (gs.at[0], gr.at[0]), sibling)]
        pump()
        for copy in hop:
            copy.wait()
        tot[...] = tot[...] + trecv[0]
        hop = [send(tot.at[:, :, 1 - x], trecv.at[1, :, :, 0], (gs.at[1], gr.at[1]), device(z, y, 1 - x, c))]
        sends.extend(hop)
        pump()
        for copy in hop:
            copy.wait_recv()
        tot[:, :, x] = tot[:, :, x] + trecv[1, :, :, 0]
        hop = [send(tot.at[:, 1 - y, x], trecv.at[2, :, 0, 0], (gs.at[2], gr.at[2]), device(z, 1 - y, x, c))]
        sends.extend(hop)
        back.wait_recv()
        far_input = local(in_recv, out_far, os.at[1])
        pump()
        for copy in hop:
            copy.wait_recv()
        tot[:, y, x] = tot[:, y, x] + trecv[2, :, 0, 0]
        hop = []
        for k in (1, 2, 3):
            other = lax.rem(z + k, 4)
            hop.append(send(tot.at[other, y, x], trecv.at[3, k, 0, 0], (gs.at[2 + k], gr.at[2 + k]), device(other, y, x, c)))
        sends.extend(hop)
        while active:
            pump()
        for copy in hop:
            copy.wait_recv()
        summed = tot[z, y, x] + trecv[3, 1, 0, 0] + trecv[3, 2, 0, 0] + trecv[3, 3, 0, 0]
        chosen = jnp.where(c == 0, summed[:, :40], summed[:, 40:80])
        o_gm[...] = chosen[0:1]
        o_ga[...] = chosen[1:2]
        own_input.wait()
        far_input.wait()
        own_layer.wait()
        back_layer.wait_recv()
        back.wait_send()
        for copy in swapped + sends + [copy for _, copy in crossing]:
            copy.wait_send()

    pl.run_scoped(
        attention,
        pltpu.VMEM((3, 8, 1024, 128), low),
        pltpu.VMEM((2, 256, 2560), low),
        pltpu.VMEM((8, 1024, 128), low),
        pltpu.VMEM((8, 1024, 128), low),
        pltpu.VMEM((2, 1024, 128), f32),
        pltpu.VMEM((3, 1024, 640), low),
        pltpu.VMEM((1280, 1024), low),
        pltpu.VMEM((2, 256, 1280), low),
        pltpu.VMEM((256, 1280), low),
        pltpu.VMEM((256, 1280), f32),
    )


def backward_part(layer, hidden, slope, turned, down, dy, wide, weights, tiles, x_own, norm_t, heads, p, oh, cosine, sine, places):
    dma = pltpu.SemaphoreType.DMA
    low, f32 = jnp.bfloat16, jnp.float32
    shape = jax.ShapeDtypeStruct
    vmem, anywhere = pl.BlockSpec(memory_space=pltpu.VMEM), pl.BlockSpec(memory_space=pl.ANY)
    row = shape((40, 1280), f32)
    bufs = [pltpu.VMEM((6,) + v, low) for piece in BACK_PIECES for v in scatter_buffers(piece, 640).values()]
    n = 6 * len(BACK_PIECES)
    return pl.pallas_call(
        backward_kernel,
        name="backward_scatter",
        out_shape=(shape((2, 256, 1280), low), shape((256, 1280), f32), shape((256, 1280), low)) + (row,) * 6 + (shape((1, 40), f32),) * 2,
        in_specs=[anywhere] * 8 + [vmem] + [anywhere] * 5 + [vmem] * 3,
        out_specs=(anywhere,) * 3 + (vmem,) * 8,
        scratch_shapes=[
            pltpu.VMEM((SLOTS, 4, 2, 2, 80, 640), low),
            pltpu.VMEM((3, 4, 2, 2, 80, 640), low),
            pltpu.VMEM((4, 256, 640), low),
            pltpu.VMEM((2, 256, 1280), low),
            pltpu.VMEM((512, 1280), f32),
            pltpu.VMEM((2, 256, 1280), low),
            pltpu.VMEM((2, 256, 1280), low),
            pltpu.VMEM((256, 1280), low),
            pltpu.VMEM((6, 80, 640), f32),
            pltpu.VMEM((6, 40, 640), f32),
            pltpu.VMEM((4, 2, 2, 8, 128), f32),
            pltpu.VMEM((4, 4, 2, 2, 8, 128), f32),
            pltpu.VMEM((8, 1280), f32),
            dma((11,)), dma((5,)), dma((5,)), dma((n, 10)), dma((n, 10)), dma((6,)), dma((6,)), dma((6,)), dma((6,)),
            dma((2,)), dma((2,)), dma((2,)), dma((2,)), dma((2,)), dma((2,)),
        ] + bufs,
        compiler_params=pltpu.CompilerParams(
            collective_id=1, has_side_effects=True, vmem_limit_bytes=62 << 20
        ),
    )(layer, hidden.reshape(512, 1280), slope.reshape(512, 1280), turned, down, dy.reshape(512, 1280), wide, weights, tiles,
      x_own, norm_t, heads, p, oh, cosine, sine, places)


def last_kernel(*refs):
    given, made, held = refs[:11], refs[11:21], refs[21:32]
    wide, ins, outs = refs[32:]
    x = lax.axis_index("seq") // 2
    arrivals = [pltpu.make_async_copy(given[i], held[i], ins.at[i]) for i in range(11)]
    for copy in arrivals:
        copy.start()
    leaving = [pltpu.make_async_copy(held[0], made[0], outs.at[0]), pltpu.make_async_copy(held[1], made[1].at[x], outs.at[1])]
    leaving += [pltpu.make_async_copy(held[i], made[i - 1], outs.at[i]) for i in range(3, 11)]
    arrivals[2].wait()
    wide[...] = held[2][...].astype(jnp.float32)
    far = pltpu.make_async_copy(wide, made[1].at[1 - x], outs.at[2])
    far.start()
    for copy, after in zip(arrivals[:2] + arrivals[3:], leaving):
        copy.wait()
        after.start()
    for copy in leaving + [far]:
        copy.wait()


def last_part(layer, near, far, *others):
    shape = jax.ShapeDtypeStruct
    anywhere = pl.BlockSpec(memory_space=pl.ANY)
    given = (layer, near, far) + others
    made = (shape(layer.shape, layer.dtype), shape(layer.shape, near.dtype)) + tuple(shape(o.shape, o.dtype) for o in others)
    return pl.pallas_call(
        last_kernel,
        name="lay_out",
        out_shape=made,
        in_specs=[anywhere] * len(given),
        out_specs=(anywhere,) * len(made),
        scratch_shapes=[pltpu.VMEM(g.shape, g.dtype) for g in given]
        + [pltpu.VMEM(near.shape, near.dtype), pltpu.SemaphoreType.DMA((11,)), pltpu.SemaphoreType.DMA((11,))],
        compiler_params=pltpu.CompilerParams(vmem_limit_bytes=60 << 20),
    )(*given)


def body(
    inputs,
    w_query,
    w_key,
    w_value,
    w_out,
    w_up,
    w_down,
    gain_attn,
    gain_mlp,
    pad_patches,
    cotangent,
):
    contexts, patches, model_width = inputs.shape
    head_count = HEADS
    head_size = HEAD_DIM
    seq_count = lax.axis_size("seq")
    seq_rank = lax.axis_index("seq")
    token_rows = contexts * patches
    shape_heads = (contexts, patches, head_count, head_size)
    shape_flat = (contexts, patches, model_width)
    shards = (w_query, w_key, w_value, w_out, w_up, w_down, gain_attn, gain_mlp)
    gathered = (
        lax.all_gather(shards[0], ("dp", "seq"), axis=0, tiled=True),
        lax.all_gather(shards[1], ("dp", "seq"), axis=0, tiled=True),
        lax.all_gather(shards[2], ("dp", "seq"), axis=0, tiled=True),
        lax.all_gather(shards[3], ("dp", "seq"), axis=0, tiled=True),
        lax.all_gather(shards[4], ("dp", "seq"), axis=0, tiled=True),
        lax.all_gather(shards[5], ("dp", "seq"), axis=0, tiled=True),
        lax.all_gather(shards[6], ("dp", "seq"), axis=0, tiled=True),
        lax.all_gather(shards[7], ("dp", "seq"), axis=0, tiled=True),
    )
    full_q, full_k, full_v, full_o, full_up, full_down, full_ga, full_gm = gathered
    positions = seq_rank * patches + jnp.arange(patches, dtype=jnp.int32)
    cosine, sine = rope_tables(positions, head_size // 2)
    inputs_f = inputs.astype(jnp.float32).reshape(token_rows, model_width)
    gain_one = full_ga.astype(jnp.float32)
    scale_one = rms_scale(inputs_f)
    flat_attn = (inputs_f * scale_one * gain_one).astype(jnp.bfloat16)
    query_lin = jnp.dot(flat_attn, full_q, preferred_element_type=jnp.float32).reshape(shape_heads)
    key_lin = jnp.dot(flat_attn, full_k, preferred_element_type=jnp.float32).reshape(shape_heads)
    value_flat = jnp.dot(flat_attn, full_v, preferred_element_type=jnp.float32).astype(jnp.bfloat16)
    queries = rotate_pairs(query_lin, cosine, sine).astype(jnp.bfloat16)
    key_flat = rotate_pairs(key_lin, cosine, sine).astype(jnp.bfloat16)
    own_blocks = (key_flat.reshape(shape_flat), value_flat.reshape(shape_flat))
    kept = []
    sources = []
    current = own_blocks
    for offset in range(seq_count):
        if offset > 0:
            current = shifted((current[0], current[1]), "seq", 1)
        kept.append(current)
        sources.append(seq_rank - offset)
    stats = []
    for block_pair, source_idx in zip(kept, sources):
        stats.append(
            block_forward(
                queries,
                block_pair[0].reshape(shape_heads),
                block_pair[1].reshape(shape_heads),
                source_idx,
                positions,
                pad_patches,
                patches,
            )
        )
    peaks = jnp.stack([entry[0] for entry in stats])
    masses = jnp.stack([entry[1] for entry in stats])
    partials = jnp.stack([entry[2] for entry in stats])
    summit = jnp.max(peaks, axis=0)
    weights_blk = jnp.exp(peaks - summit[None])
    total = jnp.sum(weights_blk * masses, axis=0)
    attended = (
        jnp.sum(jnp.swapaxes(weights_blk, 2, 3)[..., None] * partials, axis=0)
        / jnp.swapaxes(total, 1, 2)[..., None]
    )
    attn_low = attended.astype(jnp.bfloat16).reshape(token_rows, model_width)
    branch = jnp.dot(attn_low, full_o, preferred_element_type=jnp.float32)
    hidden = inputs_f + branch
    gain_two = full_gm.astype(jnp.float32)
    scale_two = rms_scale(hidden)
    norm_mlp = (hidden * scale_two * gain_two).astype(jnp.bfloat16)
    upper = jnp.dot(norm_mlp, full_up, preferred_element_type=jnp.float32)
    active = jax.nn.silu(upper).astype(jnp.bfloat16)
    mlp_out = jnp.dot(active, full_down, preferred_element_type=jnp.float32)
    layer_out = (hidden + mlp_out).astype(jnp.bfloat16).reshape(shape_flat)
    back_q, back_k, back_v, back_o, back_up, back_down, back_ga, back_gm = gathered
    cot_low = cotangent.reshape(token_rows, model_width)
    cot_full = cot_low.astype(jnp.float32)
    grad_downw = jnp.dot(active.T, cot_low, preferred_element_type=jnp.float32)
    grad_active = jnp.dot(cot_low, back_down.T, preferred_element_type=jnp.float32)
    sigmoid_up = jax.nn.sigmoid(upper)
    grad_upper = (grad_active * sigmoid_up * (1.0 + upper * (1.0 - sigmoid_up))).astype(
        jnp.bfloat16
    )
    grad_upw = jnp.dot(norm_mlp.T, grad_upper, preferred_element_type=jnp.float32)
    grad_norm_mlp = jnp.dot(grad_upper, back_up.T, preferred_element_type=jnp.float32)
    grad_from_mlp, grad_gain_two = rms_back(
        hidden, scale_two, back_gm.astype(jnp.float32), grad_norm_mlp
    )
    grad_hidden = cot_full + grad_from_mlp
    hid_low = grad_hidden.astype(jnp.bfloat16)
    grad_outw = jnp.dot(attn_low.T, hid_low, preferred_element_type=jnp.float32)
    grad_attn = jnp.dot(hid_low, back_o.T, preferred_element_type=jnp.float32).astype(jnp.bfloat16)
    grad_attn_f = grad_attn.astype(jnp.float32).reshape(shape_heads)
    delta = jnp.swapaxes(jnp.sum(grad_attn_f * attended, axis=-1), 1, 2)
    grad_queries = jnp.zeros(shape_heads, jnp.float32)
    carried = (jnp.zeros(shape_flat, jnp.float32), jnp.zeros(shape_flat, jnp.float32))
    for offset in reversed(range(seq_count)):
        block_pair = kept[offset]
        part_q, part_k, part_v = block_backward(
            queries,
            block_pair[0].reshape(shape_heads),
            block_pair[1].reshape(shape_heads),
            sources[offset],
            positions,
            pad_patches,
            patches,
            summit,
            total,
            delta,
            grad_attn_f,
        )
        grad_queries = grad_queries + part_q
        carried = (carried[0] + part_k.reshape(shape_flat), carried[1] + part_v.reshape(shape_flat))
        if offset > 0:
            carried = (
                shifted(carried[0].astype(jnp.bfloat16), "seq", -1).astype(jnp.float32),
                shifted(carried[1].astype(jnp.bfloat16), "seq", -1).astype(jnp.float32),
            )
    grad_keys, grad_values = carried
    scale_factor = head_size ** (-0.5)
    grad_qlin = (
        rotate_back(grad_queries * scale_factor, cosine, sine)
        .astype(jnp.bfloat16)
        .reshape(token_rows, model_width)
    )
    grad_klin = (
        rotate_back(grad_keys.reshape(shape_heads) * scale_factor, cosine, sine)
        .astype(jnp.bfloat16)
        .reshape(token_rows, model_width)
    )
    grad_vlin = grad_values.astype(jnp.bfloat16).reshape(token_rows, model_width)
    grad_qw = jnp.dot(flat_attn.T, grad_qlin, preferred_element_type=jnp.float32)
    grad_kw = jnp.dot(flat_attn.T, grad_klin, preferred_element_type=jnp.float32)
    grad_vw = jnp.dot(flat_attn.T, grad_vlin, preferred_element_type=jnp.float32)
    grad_norm_attn = jnp.dot(grad_qlin, back_q.T, preferred_element_type=jnp.float32)
    grad_norm_attn = grad_norm_attn + jnp.dot(
        grad_klin, back_k.T, preferred_element_type=jnp.float32
    )
    grad_norm_attn = grad_norm_attn + jnp.dot(
        grad_vlin, back_v.T, preferred_element_type=jnp.float32
    )
    grad_from_attn, grad_gain_one = rms_back(
        inputs_f, scale_one, back_ga.astype(jnp.float32), grad_norm_attn
    )
    grad_input = (grad_hidden + grad_from_attn).reshape(shape_flat)
    totals = (
        lax.psum_scatter(grad_qw, ("dp", "seq"), scatter_dimension=0, tiled=True),
        lax.psum_scatter(grad_kw, ("dp", "seq"), scatter_dimension=0, tiled=True),
        lax.psum_scatter(grad_vw, ("dp", "seq"), scatter_dimension=0, tiled=True),
        lax.psum_scatter(grad_outw, ("dp", "seq"), scatter_dimension=0, tiled=True),
        lax.psum_scatter(grad_upw, ("dp", "seq"), scatter_dimension=0, tiled=True),
        lax.psum_scatter(grad_downw, ("dp", "seq"), scatter_dimension=0, tiled=True),
        lax.psum_scatter(grad_gain_one, ("dp", "seq"), scatter_dimension=0, tiled=True),
        lax.psum_scatter(grad_gain_two, ("dp", "seq"), scatter_dimension=0, tiled=True),
    )
    return (
        layer_out,
        grad_input,
        totals[0],
        totals[1],
        totals[2],
        totals[3],
        totals[4],
        totals[5],
        totals[6],
        totals[7],
    )


def tables(length):
    places = np.arange(length, dtype=np.float32)[:, None]
    freqs = np.float32(10000.0) ** (-np.arange(40, dtype=np.float32) / np.float32(40))
    angles = places * freqs[None]
    wide = ((0, 0), (0, 48))
    moves = np.zeros((2, 4, 256, 256), np.float32)
    for g in range(4):
        for head in range(2):
            for entry in range(80):
                base = 80 * (2 * g + head) - 128 * g
                other = entry + 40 if entry < 40 else entry - 40
                moves[0, g, base + entry, 128 * head + entry] = 1.0
                moves[1, g, base + other, 128 * head + entry] = -1.0 if entry < 40 else 1.0
    cosine, sine = (np.pad(np.tile(f(angles), (1, 2)), wide) for f in (np.cos, np.sin))
    return jnp.asarray(cosine), jnp.asarray(sine), jnp.asarray(moves, jnp.bfloat16)


def fast_body(
    inputs, w_query, w_key, w_value, w_out, w_up, w_down, gain_attn, gain_mlp, pad_patches, cotangent
):
    moves = tables(1024)
    tile = jnp.pad(jnp.stack([gain_attn, gain_mlp]).astype(jnp.float32), ((0, 6), (0, 88)))
    weights, wide, tiles, x_own, dy_own, norm_t, heads, p, oh, hidden, layer, slope, turned, down = forward_part(
        inputs, cotangent, (w_query, w_key, w_value, w_out, w_up, w_down), tile, pad_patches, *moves
    )
    results = last_part(*backward_part(
        layer, hidden, slope, turned, down, dy_own, wide, weights, tiles, x_own, norm_t, heads, p, oh, *moves
    ))
    return results[:8] + (results[8].reshape(40), results[9].reshape(40))


def solution(mesh):
    placed = (
        P("dp", "seq", None),
        P(("dp", "seq"), None),
        P(("dp", "seq"), None),
        P(("dp", "seq"), None),
        P(("dp", "seq"), None),
        P(("dp", "seq"), None),
        P(("dp", "seq"), None),
        P(("dp", "seq")),
        P(("dp", "seq")),
        P("dp"),
        P("dp", "seq", None),
    )
    return jax.shard_map(
        fast_body if dict(mesh.shape) == {"dp": 8, "seq": 4} else body,
        mesh=mesh,
        in_specs=placed,
        out_specs=(
            P("dp", "seq", None),
            P("dp", "seq", None),
            P(("dp", "seq"), None),
            P(("dp", "seq"), None),
            P(("dp", "seq"), None),
            P(("dp", "seq"), None),
            P(("dp", "seq"), None),
            P(("dp", "seq"), None),
            P(("dp", "seq")),
            P(("dp", "seq")),
        ),
        check_vma=False,
    )
```

profile of v0, /device:TPU:0, one launch (start us, length us, event | category | flops | bytes accessed | tf_op | source)
XLA Modules:
  0.0 246.7 jit_solution(12725988337402028251)
XLA Ops:
  0.6 1.3 fusion.6.refs_8_
  1.9 120.8 %gather_forward.1 = (bf16[3,4,2,2,80,640]{5,4,3,2,1,0:T(8,128)(2,1)}, bf16[3,2,4,2,2,80,640]{6,5,4,3,2,1,0:T(8,128)(2,1)}, f32[4,2,2,2,8,128]{5,4,3,2,1,0:T(8,12...) custom-call(bf16[2,256,1280]{2,1,0:T(8,128)(2,1)} %refs_0_.1, ...), custom_call_target="tpu_custom_call" | custom-call | tf_op jit(solution)/shard_map/gather_forward/pallas_call | solution.py:558
  122.7 119.4 %backward_scatter.1 = (bf16[2,256,1280]{2,1,0:T(8,128)(2,1)}, f32[256,1280]{1,0:T(8,128)}, bf16[256,1280]{1,0:T(8,128)(2,1)}, f32[40,1280]{1,0:T(8,128)}, f32[40...) custom-call(bf16[2,256,1280]{2,1,0:T(8,128)(2,1)} %get-tuple-element, ...), custom_call_target="tpu_custom_call" | custom-call | tf_op jit(solution)/shard_map/backward_scatter/pallas_call | solution.py:1083
  242.1 4.5 %lay_out.1 = (bf16[2,256,1280]{2,1,0:T(8,128)(2,1)}, f32[2,256,1280]{2,1,0:T(8,128)}, f32[40,1280]{1,0:T(8,128)}, f32[40,1280]{1,0:T(8,128)}, f32[40,1280]{1,0:T...) custom-call(bf16[2,256,1280]{2,1,0:T(8,128)(2,1)} %get-tuple-element, ...), custom_call_target="tpu_custom_call" | custom-call | tf_op jit(solution)/shard_map/lay_out/pallas_call | solution.py:1138
where the time goes:
time: 247 us
  Pallas kernels  245 us (99%)
    pallas_call x1, Pallas kernels, forward_part(): pl.pallas_call(forward_kernel, name='gather_forward', out_shape=(shape((3...  121 us
    pallas_call x1, Pallas kernels, backward_part(): pl.pallas_call(backward_kernel, name='backward_scatter', out_shape=(shape...  119 us

commit v1 on v0

--- a/solution.py
+++ b/solution.py
@@ -356,7 +356,7 @@
             swap(inputs, held)
             if t == 2:
                 swap(inputs, held)
-        if 5 <= t < 9:
+        if 7 <= t < 11:
             swap(cot, held_dy)
         if 0 <= t - 3 < count:
             steps[t - 3].arrive(2)

time: 247 us -> 248 us (level)
  no operation moved by 1% of the time
where the time goes in v1:
time: 248 us
  Pallas kernels  246 us (99%)
    pallas_call x1, Pallas kernels, forward_part(): pl.pallas_call(forward_kernel, name='gather_forward', out_shape=(shape((3...  121 us
    pallas_call x1, Pallas kernels, backward_part(): pl.pallas_call(backward_kernel, name='backward_scatter', out_shape=(shape...  120 us

profile of v1, /device:TPU:0, one launch (start us, length us, event | category | flops | bytes accessed | tf_op | source)
XLA Modules:
  0.0 247.7 jit_solution(16706778719402642116)
XLA Ops:
  0.6 1.3 fusion.6.refs_8_
  1.9 120.7 %gather_forward.1 = (bf16[3,4,2,2,80,640]{5,4,3,2,1,0:T(8,128)(2,1)}, bf16[3,2,4,2,2,80,640]{6,5,4,3,2,1,0:T(8,128)(2,1)}, f32[4,2,2,2,8,128]{5,4,3,2,1,0:T(8,12...) custom-call(bf16[2,256,1280]{2,1,0:T(8,128)(2,1)} %refs_0_.1, ...), custom_call_target="tpu_custom_call" | custom-call | tf_op jit(solution)/shard_map/gather_forward/pallas_call | solution.py:558
  122.6 120.4 %backward_scatter.1 = (bf16[2,256,1280]{2,1,0:T(8,128)(2,1)}, f32[256,1280]{1,0:T(8,128)}, bf16[256,1280]{1,0:T(8,128)(2,1)}, f32[40,1280]{1,0:T(8,128)}, f32[40...) custom-call(bf16[2,256,1280]{2,1,0:T(8,128)(2,1)} %get-tuple-element, ...), custom_call_target="tpu_custom_call" | custom-call | tf_op jit(solution)/shard_map/backward_scatter/pallas_call | solution.py:1083
  243.0 4.5 %lay_out.1 = (bf16[2,256,1280]{2,1,0:T(8,128)(2,1)}, f32[2,256,1280]{2,1,0:T(8,128)}, f32[40,1280]{1,0:T(8,128)}, f32[40,1280]{1,0:T(8,128)}, f32[40,1280]{1,0:T...) custom-call(bf16[2,256,1280]{2,1,0:T(8,128)(2,1)} %get-tuple-element, ...), custom_call_target="tpu_custom_call" | custom-call | tf_op jit(solution)/shard_map/lay_out/pallas_call | solution.py:1138
